TPU v7x, 32 devices: a whole 2x2x4 slice. The times are simulated.
32 devices in a mesh: seq: 8 (over z, x), ch: 4 (over y, core).
Axes of the slice: x: 2, y: 2, z: 4, core: 2. Of those that a mesh axis runs over, the one named last changes fastest.
Arguments:
- bins_in: bfloat16 [8192, 1536], P('seq', 'ch'), may hold values from -6 to 6
- pre_scale: float32 [3, 1536], P(None, 'ch'), may hold values from 0.5 to 2
- pre_shift: float32 [3, 1536], P(None, 'ch'), may hold values from -1 to 1
- conv_weight: bfloat16 [3, 3, 1536, 1536], P(None, None, None, 'ch'), may hold values from -0.09375 to 0.09375
- conv_bias: float32 [3, 1536], P(None, 'ch'), may hold values from -0.5 to 0.5
Outputs:
- bins_out: bfloat16 [8192, 1536], P('seq', 'ch')
All inputs are finite; a program needn't handle non-finite values.
Results may differ from a plain program's by a relative error of at most 0.015.
Values may be sent and summed in bfloat16 or wider, within the bound.
A program may use at most 64 MiB of HBM per device.

v0:
```python
import jax
import jax.numpy as jnp
from jax import lax
from jax.sharding import PartitionSpec as P

LAYERS = 3
FIRST_SPACING1 = 64
SECOND_SPACING2 = 512
THIRD_SPACING3 = 4096


def shifted(array, axis, by):
    size = lax.axis_size(axis)
    pairs = [(i, i + by) for i in range(size) if 0 <= i + by < size]
    return lax.ppermute(array, axis, pairs)


def neighbours(source, dilation, bin_rows):
    if dilation < bin_rows:
        to_next = source[bin_rows - dilation :]
        to_prev = source[:dilation]
        hop_count = 1
    else:
        to_next = source
        to_prev = source
        hop_count = dilation // bin_rows
    lower_rim = shifted(to_next, "seq", hop_count)
    upper_rim = shifted(to_prev, "seq", -hop_count)
    return (lower_rim, upper_rim)


def arrange(lower_rim, centre, upper_rim, dilation, bin_rows):
    if dilation < bin_rows:
        extended = jnp.concatenate([lower_rim, centre, upper_rim], axis=0)
        return (extended[:bin_rows], centre, extended[2 * dilation : 2 * dilation + bin_rows])
    return (lower_rim, centre, upper_rim)


def per_device(bins_in, pre_scale, pre_shift, conv_weight, conv_bias):
    layer_spacings = (FIRST_SPACING1, SECOND_SPACING2, THIRD_SPACING3)
    bin_rows = bins_in.shape[0]
    stream = bins_in
    for layer_index in range(LAYERS):
        dilation = layer_spacings[layer_index]
        activated = jax.nn.gelu(
            stream.astype(jnp.float32) * pre_scale[layer_index] + pre_shift[layer_index],
            approximate=False,
        ).astype(jnp.bfloat16)
        weights = conv_weight[layer_index]
        gathered = lax.all_gather(activated, "ch", axis=1, tiled=True)
        lower_rim, upper_rim = neighbours(gathered, dilation, bin_rows)
        tap_inputs = arrange(lower_rim, gathered, upper_rim, dilation, bin_rows)
        summed = jnp.dot(tap_inputs[0], weights[0], preferred_element_type=jnp.float32)
        summed = summed + jnp.dot(tap_inputs[1], weights[1], preferred_element_type=jnp.float32)
        summed = summed + jnp.dot(tap_inputs[2], weights[2], preferred_element_type=jnp.float32)
        stream = (stream.astype(jnp.float32) + summed + conv_bias[layer_index]).astype(jnp.bfloat16)
    return stream


def solution(mesh):
    return jax.shard_map(
        per_device,
        mesh=mesh,
        in_specs=(
            P("seq", "ch"),
            P(None, "ch"),
            P(None, "ch"),
            P(None, None, None, "ch"),
            P(None, "ch"),
        ),
        out_specs=P("seq", "ch"),
        check_vma=False,
    )
```

profile of v0, /device:TPU:0, one launch (start us, length us, event | category | flops | bytes accessed | tf_op | source)
XLA Modules:
  0.0 363.3 jit_solution(14618587628513160719)
XLA Ops:
  6.5 0.9 slice_reduce_fusion.1
  7.4 5.3 %fusion.12 = bf16[1024,384]{1,0:T(8,128)(2,1)} fusion(bf16[1024,384]{1,0:T(8,128)(2,1)} %param.5, f32[384]{0:T(512)S(1)} %get-tuple-element.12, f32[384]{0:T(512)S(1)} %get-tuple-element.23), kind=kLoop, calls=%fused_computation.25 | loop fusion | flops 26738688 | bytes 1575936 | tf_op jit(solution)/shard_map/convert_element_type | solution.py:48
  12.7 0.0 all-gather.4.cloned.1.call-update
  12.8 0.0 all-gather.6.cloned.1.call-start
  12.9 31.3 %all-gather.4.cloned.1.call-done = bf16[1024,1536]{1,0:T(8,128)(2,1)} async-done(((bf16[1024,384]{1,0:T(8,128)(2,1)}), bf16[1024,1536]{1,0:T(8,128)(2,1)}) %all-gather.4.cloned.1.call-update) | async-done | bytes 3145744 | tf_op jit(solution)/shard_map/all_gather | solution.py:50
  44.1 1.0 fusion.117
  45.2 3.4 collective-permute-start
  48.6 1.6 collective-permute-start.1
  50.1 4.0 %fusion.94 = f32[1024,384]{1,0:T(8,128)S(1)} fusion(bf16[1024,1536]{1,0:T(8,128)(2,1)} %all-gather.4.cloned.1.call-done, bf16[3,3,1536,384]{3,2,1,0:T(8,128)(2,1)} %param.8), kind=kOutput, calls=%fused_computation.107 | convolution fusion | flops 1207959552 | bytes 5898240 | tf_op jit(solution)/shard_map/dot_general | solution.py:54
  54.1 0.0 copy-start.1
  54.2 3.1 fusion.6
  57.3 0.2 collective-permute-done.1
  57.5 7.9 %fusion.26 = (bf16[1024,384]{1,0:T(8,128)(2,1)}, bf16[1024,384]{1,0:T(8,128)(2,1)S(1)}) fusion(f32[384]{0:T(512)S(1)} %get-tuple-element.13, f32[384]{0:T(512)S(1)} %get-tuple-element.22, f32[384]{0:T(512)S(1)} %get-tuple-element.6, bf16[3,3,1536,384]{3,2,1,0:T(8,128)(2,1)} %param.8, bf16[64,1536]{1,0:T(8,128)(2,1)S(1)} %collective-permute-done.1, ...), kind=kOutput, calls=%fused_computation.39 | convolution fusion | flops 1243348992 | bytes 10031616 | tf_op jit(solution)/shard_map/dot_general | solution.py:55
  65.4 0.0 all-gather.6.cloned.1.call-update
  65.4 0.0 all-gather.8.cloned.1.call-start
  65.4 29.6 %all-gather.6.cloned.1.call-done = bf16[1024,1536]{1,0:T(8,128)(2,1)} async-done(((bf16[1024,384]{1,0:T(8,128)(2,1)}), bf16[1024,1536]{1,0:T(8,128)(2,1)}) %all-gather.6.cloned.1.call-update) | async-done | bytes 3145744 | tf_op jit(solution)/shard_map/all_gather | solution.py:50
  95.1 2.2 fusion.116
  97.3 3.5 collective-permute-start.2
  100.8 1.5 collective-permute-start.3
  102.3 3.1 fusion.90
  105.3 63.1 %collective-permute-done.2 = bf16[512,1536]{1,0:T(8,128)(2,1)S(1)} collective-permute-done((bf16[512,1536]{1,0:T(8,128)(2,1)S(1)}, bf16[512,1536]{1,0:T(8,128)(2,1)S(1)}, u32[]{:S(2)}, u32[]{:S(2)}) %collective-permute-start.2) | collective-permute-done | bytes 1572896 | tf_op jit(solution)/shard_map/ppermute | solution.py:15
  168.4 3.0 fusion.2
  171.5 7.5 %fusion.40 = (bf16[1024,384]{1,0:T(8,128)(2,1)}, bf16[1024,384]{1,0:T(8,128)(2,1)S(1)}) fusion(f32[384]{0:T(512)S(1)} %get-tuple-element.11, f32[384]{0:T(512)S(1)} %get-tuple-element.24, f32[384]{0:T(512)S(1)} %get-tuple-element.7, bf16[3,3,1536,384]{3,2,1,0:T(8,128)(2,1)} %param.8, bf16[512,1536]{1,0:T(8,128)(2,1)S(1)} %collective-permute-done.3, ...), kind=kOutput, calls=%fused_computation.53 | convolution fusion | flops 1243348992 | bytes 11407872 | tf_op jit(solution)/shard_map/dot_general | solution.py:55
  179.0 0.0 all-gather.8.cloned.1.call-update
  179.0 28.8 %all-gather.8.cloned.1.call-done = bf16[1024,1536]{1,0:T(8,128)(2,1)} async-done(((bf16[1024,384]{1,0:T(8,128)(2,1)}), bf16[1024,1536]{1,0:T(8,128)(2,1)}) %all-gather.8.cloned.1.call-update) | async-done | bytes 3145744 | tf_op jit(solution)/shard_map/all_gather | solution.py:50
  207.7 4.5 %collective-permute-start.4 = (bf16[1024,1536]{1,0:T(8,128)(2,1)}, bf16[1024,1536]{1,0:T(8,128)(2,1)S(1)}, u32[]{:S(2)}, u32[]{:S(2)}) collective-permute-start(bf16[1024,1536]{1,0:T(8,128)(2,1)} %all-gather.8.cloned.1.call-done), channel_id=1, source_target_pairs={{0,16},{4,20},{8,24},{12,28},{1,17},{5,21},{9,25},{13,29},{2,18},{... | collective-permute-start | bytes 9437192 | tf_op jit(solution)/shard_map/ppermute | solution.py:15
  212.2 1.3 collective-permute-start.5
  213.5 4.0 %fusion.85 = f32[1024,384]{1,0:T(8,128)S(1)} fusion(bf16[1024,1536]{1,0:T(8,128)(2,1)} %all-gather.8.cloned.1.call-done, bf16[3,3,1536,384]{3,2,1,0:T(8,128)(2,1)} %param.8), kind=kOutput, calls=%fused_computation.98 | convolution fusion | flops 1207959552 | bytes 5898240 | tf_op jit(solution)/shard_map/dot_general | solution.py:54
  217.5 62.6 %collective-permute-done.4 = bf16[1024,1536]{1,0:T(8,128)(2,1)S(1)} collective-permute-done((bf16[1024,1536]{1,0:T(8,128)(2,1)}, bf16[1024,1536]{1,0:T(8,128)(2,1)S(1)}, u32[]{:S(2)}, u32[]{:S(2)}) %collective-permute-start.4) | collective-permute-done | bytes 3145760 | tf_op jit(solution)/shard_map/ppermute | solution.py:15
  280.1 3.0 fusion.87
  283.2 69.4 %collective-permute-done.5 = bf16[1024,1536]{1,0:T(8,128)(2,1)S(1)} collective-permute-done((bf16[1024,1536]{1,0:T(8,128)(2,1)}, bf16[1024,1536]{1,0:T(8,128)(2,1)S(1)}, u32[]{:S(2)}, u32[]{:S(2)}) %collective-permute-start.5) | collective-permute-done | bytes 3145760 | tf_op jit(solution)/shard_map/ppermute | solution.py:15
  352.6 4.1 %fusion.49 = bf16[1024,384]{1,0:T(8,128)(2,1)} fusion(bf16[1024,384]{1,0:T(8,128)(2,1)S(1)} %get-tuple-element.21, f32[1024,384]{1,0:T(8,128)S(1)} %fusion.87, f32[1024,384]{1,0:T(8,128)S(1)} %fusion.85, bf16[1024,1536]{1,0:T(8,128)(2,1)S(1)} %collective-permute-done.5, bf16[3,3,1536,384]{3,2,1,0:T(8,128)(2,1)} %param.8, f32[384]{0:T(512)S(1)} %get-tuple-element.5), kind=kOutput, calls=%fused_computation.62 | convolution fusion | flops 1210318848 | bytes 9045504 | tf_op jit(solution)/shard_map/dot_general | solution.py:55
  (11 shorter events, 0.1 us)
Async XLA Ops:
  6.5 6.3 %copy-start.3 = (f32[3,384]{1,0:T(4,128)S(1)}, f32[3,384]{1,0:T(4,128)}, u32[]{:S(2)}) copy-start(f32[3,384]{1,0:T(4,128)} %param.9) | copy-start | bytes 13828
  6.5 37.6 %all-gather.4.cloned.1.call-start = ((), (), s32[]{:S(2)}) async-start(), calls=%async_computation | async-start | bytes 3932160 | tf_op jit(solution)/shard_map/all_gather | solution.py:50
  12.8 82.3 %all-gather.6.cloned.1.call-start = ((), (), s32[]{:S(2)}) async-start(), calls=%async_computation.1 | async-start | bytes 3932160 | tf_op jit(solution)/shard_map/all_gather | solution.py:50
  45.2 9.0 %collective-permute-start = (bf16[64,1536]{1,0:T(8,128)(2,1)S(1)}, bf16[64,1536]{1,0:T(8,128)(2,1)S(1)}, u32[]{:S(2)}, u32[]{:S(2)}) collective-permute-start(bf16[64,1536]{1,0:T(8,128)(2,1)S(1)} %get-tuple-element.17), channel_id=1, source_target_pairs={{0,4},{4,8},{8,12},{12,16},{16,20},{20,24},{24,28},{1,5},{5,9},{9,... | collective-permute-start | bytes 589832 | tf_op jit(solution)/shard_map/ppermute | solution.py:15
  48.6 5.6 %copy-start.2 = (bf16[1024,1536]{1,0:T(8,128)(2,1)S(1)}, bf16[1024,1536]{1,0:T(8,128)(2,1)}, u32[]{:S(2)}) copy-start(bf16[1024,1536]{1,0:T(8,128)(2,1)} %all-gather.4.cloned.1.call-done) | copy-start | bytes 9437188
  48.6 8.9 %collective-permute-start.1 = (bf16[64,1536]{1,0:T(8,128)(2,1)S(1)}, bf16[64,1536]{1,0:T(8,128)(2,1)S(1)}, u32[]{:S(2)}, u32[]{:S(2)}) collective-permute-start(bf16[64,1536]{1,0:T(8,128)(2,1)S(1)} %get-tuple-element.16), channel_id=1, source_target_pairs={{4,0},{8,4},{12,8},{16,12},{20,16},{24,20},{28,24},{5,1},{9,5},{13... | collective-permute-start | bytes 589832 | tf_op jit(solution)/shard_map/ppermute | solution.py:15
  54.1 3.4 copy-start.1
  65.4 142.3 %all-gather.8.cloned.1.call-start = ((), (), s32[]{:S(2)}) async-start(), calls=%async_computation.2 | async-start | bytes 3932160 | tf_op jit(solution)/shard_map/all_gather | solution.py:50
  95.1 7.2 %copy-start = (bf16[1024,1536]{1,0:T(8,128)(2,1)S(1)}, bf16[1024,1536]{1,0:T(8,128)(2,1)}, u32[]{:S(2)}) copy-start(bf16[1024,1536]{1,0:T(8,128)(2,1)} %all-gather.6.cloned.1.call-done) | copy-start | bytes 9437188
  97.3 71.1 %collective-permute-start.2 = (bf16[512,1536]{1,0:T(8,128)(2,1)S(1)}, bf16[512,1536]{1,0:T(8,128)(2,1)S(1)}, u32[]{:S(2)}, u32[]{:S(2)}) collective-permute-start(bf16[512,1536]{1,0:T(8,128)(2,1)S(1)} %get-tuple-element.15), channel_id=1, source_target_pairs={{0,4},{4,8},{8,12},{12,16},{16,20},{20,24},{24,28},{1,5},{5,9},{9,... | collective-permute-start | bytes 4718600 | tf_op jit(solution)/shard_map/ppermute | solution.py:15
  100.8 70.7 %collective-permute-start.3 = (bf16[512,1536]{1,0:T(8,128)(2,1)S(1)}, bf16[512,1536]{1,0:T(8,128)(2,1)S(1)}, u32[]{:S(2)}, u32[]{:S(2)}) collective-permute-start(bf16[512,1536]{1,0:T(8,128)(2,1)S(1)} %get-tuple-element.14), channel_id=1, source_target_pairs={{4,0},{8,4},{12,8},{16,12},{20,16},{24,20},{28,24},{5,1},{9,5},{13... | collective-permute-start | bytes 4718600 | tf_op jit(solution)/shard_map/ppermute | solution.py:15
  207.7 72.4 %collective-permute-start.4 = (bf16[1024,1536]{1,0:T(8,128)(2,1)}, bf16[1024,1536]{1,0:T(8,128)(2,1)S(1)}, u32[]{:S(2)}, u32[]{:S(2)}) collective-permute-start(bf16[1024,1536]{1,0:T(8,128)(2,1)} %all-gather.8.cloned.1.call-done), channel_id=1, source_target_pairs={{0,16},{4,20},{8,24},{12,28},{1,17},{5,21},{9,25},{13,29},{2,18},{... | collective-permute-start | bytes 9437192 | tf_op jit(solution)/shard_map/ppermute | solution.py:15
  212.2 140.4 %collective-permute-start.5 = (bf16[1024,1536]{1,0:T(8,128)(2,1)}, bf16[1024,1536]{1,0:T(8,128)(2,1)S(1)}, u32[]{:S(2)}, u32[]{:S(2)}) collective-permute-start(bf16[1024,1536]{1,0:T(8,128)(2,1)} %all-gather.8.cloned.1.call-done), channel_id=1, source_target_pairs={{16,0},{20,4},{24,8},{28,12},{17,1},{21,5},{25,9},{29,13},{18,2},{... | collective-permute-start | bytes 9437192 | tf_op jit(solution)/shard_map/ppermute | solution.py:15
Sparse Core Ops, SparseCore 0:
  12.9 31.1 all-gather.3
  65.5 29.5 all-gather.5
  179.1 28.5 all-gather.7
where the time goes:
time: 364 us; the launch traced here: 363 us
  waiting for transfers between devices  285 us (78%)
  matrix products  39.7 us (11%)
  starting transfers between devices  15.8 us (4%)
  between operations  13.2 us (4%)
  other arithmetic  5.32 us (1%)
  local copies, waits for them, and re-layouts  4.22 us (1%)
    ppermute x6, waiting for transfers between devices, shifted(): return lax.ppermute(array, axis, pairs)  195 us
    all_gather x3, waiting for transfers between devices, per_device(): gathered = lax.all_gather(activated, 'ch', axis=1, tiled=True)  89.6 us
    dot_general x3, matrix products, per_device(): jnp.dot(tap_inputs[2], weights[2], preferred_element_type=jnp.float32)  19.4 us
    ppermute x6, starting transfers between devices, shifted(): return lax.ppermute(array, axis, pairs)  15.7 us
    dot_general x3, matrix products, per_device(): jnp.dot(tap_inputs[1], weights[1], preferred_element_type=jnp.float32)  11 us
    dot_general x3, matrix products, per_device(): jnp.dot(tap_inputs[0], weights[0], preferred_element_type=jnp.float32)  9.21 us
  transfers between devices with their start and end apart: 9, of which 7 were waited for; matrix products, arithmetic and copies ran while one was open for 6% of the time, Pallas kernels for 0%

commit v1 on v0

v1 whole, which is shorter than its diff:
```python
import functools

import jax
import jax.numpy as jnp
from jax import lax
from jax.experimental import pallas as pl
from jax.experimental.pallas import tpu as pltpu
from jax.sharding import PartitionSpec as P

LAYERS = 3
SPACINGS = (64, 512, 4096)
PIECES = 4
MESH = pl.DeviceIdType.MESH
INV_SQRT2 = 0.7071067811865476


def kernel(
    n, x_ref, scale_ref, shift_ref, w_hbm, bias_ref, out_ref,
    full, w, acc, part, up_out, down_out, low_in, high_in,
    w_sem, core_send, core_recv, y_send, y_recv, fwd_send, fwd_recv,
    up_send, up_recv, down_send, down_recv,
):
    rows, width = x_ref.shape
    piece = rows // PIECES
    s = lax.axis_index("seq")
    c = lax.axis_index("ch")
    core = c + 1 - 2 * lax.rem(c, 2)
    across = lax.rem(c + 2, 4)
    hops = [max(1, d // rows) for d in SPACINGS]
    rims = [min(d, rows) for d in SPACINGS]
    starts = [sum(rims[:l]) for l in range(LAYERS)]
    has_up = [s + h < n for h in hops]
    has_down = [s >= h for h in hops]

    def columns(index):
        return pl.ds(pl.multiple_of(index * width, width), width)

    def span(j):
        return pl.ds(j * piece, piece)

    barrier = pltpu.get_barrier_semaphore()
    pl.semaphore_signal(barrier, inc=1, device_id={"ch": core}, device_id_type=MESH)
    pl.semaphore_signal(barrier, inc=1, device_id={"ch": across}, device_id_type=MESH)
    greeted = sorted(set(hops))
    for h in greeted:
        @pl.when(s + h < n)
        def _():
            pl.semaphore_signal(barrier, inc=1, device_id={"seq": s + h}, device_id_type=MESH)

        @pl.when(s >= h)
        def _():
            pl.semaphore_signal(barrier, inc=1, device_id={"seq": s - h}, device_id_type=MESH)

    w_copies = [pltpu.make_async_copy(w_hbm.at[l], w.at[l], w_sem.at[l]) for l in range(LAYERS)]
    for copy in w_copies:
        copy.start()

    def activate(l, j, value):
        z = value * scale_ref[l : l + 1, :] + shift_ref[l : l + 1, :]
        gelu = 0.5 * z * (1.0 + lax.erf(z * INV_SQRT2))
        full[l, span(j), columns(c)] = gelu.astype(jnp.bfloat16)
        acc[span(j), :] = value + bias_ref[l : l + 1, :]

    def block(l, j, owner):
        return full.at[l, span(j), columns(owner)]

    def core_copy(l, j):
        ref = block(l, j, c)
        return pltpu.make_async_remote_copy(
            ref, ref, core_send.at[l, j], core_recv.at[l, j],
            device_id={"ch": core}, device_id_type=MESH)

    def y_copy(l, j):
        ref = block(l, j, c)
        return pltpu.make_async_remote_copy(
            ref, ref, y_send.at[l, j], y_recv.at[l, j],
            device_id={"ch": across}, device_id_type=MESH)

    def fwd_copy(l, j):
        ref = block(l, j, across)
        return pltpu.make_async_remote_copy(
            ref, ref, fwd_send.at[l, j], fwd_recv.at[l, j],
            device_id={"ch": core}, device_id_type=MESH)

    def send(l, j):
        y_copy(l, j).start()
        core_copy(l, j).start()

    def arrive(l, j):
        y_copy(l, j).wait_recv()
        fwd_copy(l, j).start()
        core_copy(l, j).wait_recv()
        fwd_copy(l, j).wait_recv()

    def rim_rows(l, p):
        size = min(piece, rims[l])
        return pl.ds(starts[l] + p * size, size)

    def up_copy(l, p):
        at = rim_rows(l, p)
        return pltpu.make_async_remote_copy(
            up_out.at[at, :], low_in.at[at, :], up_send.at[l, p], up_recv.at[l, p],
            device_id={"seq": s + hops[l]}, device_id_type=MESH)

    def down_copy(l, p):
        at = rim_rows(l, p)
        return pltpu.make_async_remote_copy(
            down_out.at[at, :], high_in.at[at, :], down_send.at[l, p], down_recv.at[l, p],
            device_id={"seq": s - hops[l]}, device_id_type=MESH)

    def send_up(l, p, value):
        @pl.when(has_up[l])
        def _():
            up_out[rim_rows(l, p), :] = value().astype(jnp.bfloat16)
            up_copy(l, p).start()

    def send_down(l, p, value):
        @pl.when(has_down[l])
        def _():
            down_out[rim_rows(l, p), :] = value().astype(jnp.bfloat16)
            down_copy(l, p).start()

    def take_low(l, p, at):
        @pl.when(has_down[l])
        def _():
            up_copy(l, p).wait_recv()
            acc[at, :] += low_in[rim_rows(l, p), :].astype(jnp.float32)

    def take_high(l, p, at):
        @pl.when(has_up[l])
        def _():
            down_copy(l, p).wait_recv()
            acc[at, :] += high_in[rim_rows(l, p), :].astype(jnp.float32)

    def product(l, j, k):
        return jnp.dot(full[l, span(j), :], w[l, k], preferred_element_type=jnp.float32)

    def step(l, j):
        arrive(l, j)
        d = SPACINGS[l]
        if d >= rows:
            send_up(l, j, lambda: product(l, j, 0))
            send_down(l, j, lambda: product(l, j, 2))
            acc[span(j), :] += product(l, j, 1)
            return

        @pl.loop(0, 3)
        def _(k):
            part[k] = product(l, j, k)

        first = j * piece
        inside = max(0, min(piece, rows - d - first))
        if inside < piece:
            send_up(l, (first + inside + d - rows) // piece, lambda: part[0, inside:piece])
        outside = max(0, min(piece, d - first))
        if outside > 0:
            send_down(l, first // piece if d > piece else 0, lambda: part[2, 0:outside])
        acc[span(j), :] += part[1]
        if inside > 0:
            acc[pl.ds(first + d, inside), :] += part[0, 0:inside]
        if outside < piece:
            acc[pl.ds(first + outside - d, piece - outside), :] += part[2, outside:piece]

    def finish(l, j):
        d = SPACINGS[l]
        first = j * piece
        size = min(piece, rims[l])
        if first < rims[l]:
            take_low(l, first // size, pl.ds(first, size))
        if first + piece > rows - rims[l]:
            at = max(first, rows - rims[l])
            take_high(l, (at - (rows - rims[l])) // size, pl.ds(at, size))
        value = acc[span(j), :].astype(jnp.bfloat16)
        if l == LAYERS - 1:
            out_ref[span(j), :] = value
        else:
            activate(l + 1, j, value.astype(jnp.float32))
            send(l + 1, j)

    activate(0, 3, x_ref[span(3), :].astype(jnp.float32))
    met = 2
    for h in greeted:
        met = met + (s + h < n).astype(jnp.int32) + (s >= h).astype(jnp.int32)
    pl.semaphore_wait(barrier, met)
    send(0, 3)
    for j in (0, 1, 2):
        activate(0, j, x_ref[span(j), :].astype(jnp.float32))
        send(0, j)

    w_copies[0].wait()
    step(0, 3)
    step(0, 0)
    step(0, 1)
    finish(0, 0)
    step(0, 2)
    finish(0, 2)
    finish(0, 1)
    finish(0, 3)

    w_copies[1].wait()
    step(1, 0)
    step(1, 2)
    finish(1, 2)
    step(1, 1)
    finish(1, 0)
    step(1, 3)
    finish(1, 3)
    finish(1, 1)

    w_copies[2].wait()
    for j in (2, 0, 3, 1):
        step(2, j)
    for j in (2, 0, 3, 1):
        finish(2, j)

    for l in range(LAYERS):
        for j in range(PIECES):
            y_copy(l, j).wait_send()
            core_copy(l, j).wait_send()
            fwd_copy(l, j).wait_send()
        for p in range(max(1, rims[l] // piece)):
            @pl.when(has_up[l])
            def _():
                up_copy(l, p).wait_send()

            @pl.when(has_down[l])
            def _():
                down_copy(l, p).wait_send()


def per_device(n, bins_in, pre_scale, pre_shift, conv_weight, conv_bias):
    rows, width = bins_in.shape
    depth = conv_weight.shape[2]
    rim_total = sum(min(d, rows) for d in SPACINGS)
    vmem = pl.BlockSpec(memory_space=pltpu.VMEM)
    pair = pltpu.SemaphoreType.DMA((LAYERS, PIECES))
    rim = pltpu.VMEM((rim_total, width), jnp.bfloat16)
    return pl.pallas_call(
        functools.partial(kernel, n),
        out_shape=jax.ShapeDtypeStruct((rows, width), jnp.bfloat16),
        in_specs=[vmem, vmem, vmem, pl.BlockSpec(memory_space=pl.ANY), vmem],
        out_specs=vmem,
        scratch_shapes=[
            pltpu.VMEM((LAYERS, rows, depth), jnp.bfloat16),
            pltpu.VMEM((LAYERS, 3, depth, width), jnp.bfloat16),
            pltpu.VMEM((rows, width), jnp.float32),
            pltpu.VMEM((3, rows // PIECES, width), jnp.float32),
            rim, rim, rim, rim,
            pltpu.SemaphoreType.DMA((LAYERS,)),
        ] + [pair] * 10,
        compiler_params=pltpu.CompilerParams(
            collective_id=0, has_side_effects=True, vmem_limit_bytes=56 * 1024 * 1024
        ),
        cost_estimate=pl.CostEstimate(
            flops=2 * rows * depth * width * 9, bytes_accessed=9 * 2 * depth * width,
            transcendentals=3 * rows * width),
    )(bins_in, pre_scale, pre_shift, conv_weight, conv_bias)


def solution(mesh):
    return jax.shard_map(
        functools.partial(per_device, mesh.shape["seq"]),
        mesh=mesh,
        in_specs=(
            P("seq", "ch"),
            P(None, "ch"),
            P(None, "ch"),
            P(None, None, None, "ch"),
            P(None, "ch"),
        ),
        out_specs=P("seq", "ch"),
        check_vma=False,
    )
```

time: 364 us -> 95.8 us (0.26)
  waiting for transfers between devices: 285 us -> 0 us
  Pallas kernels: 0 us -> 93.5 us
  matrix products: 39.7 us -> 0 us
  starting transfers between devices: 15.8 us -> 0 us
  between operations: 13.2 us -> 0.01 us
  other arithmetic: 5.32 us -> 0 us
    ppermute x6 -> x0, waiting for transfers between devices: 195 us -> none  [shifted(): return lax.ppermute(array, axis, pairs)]
    pallas_call x0 -> x1, Pallas kernels: none -> 93.5 us  [per_device(): pl.pallas_call(functools.partial(kernel, n), out_shape=jax.ShapeDtypeStru...]
    all_gather x3 -> x0, waiting for transfers between devices: 89.6 us -> none  [per_device(): gathered = lax.all_gather(activated, 'ch', axis=1, tiled=True)]
    dot_general x9 -> x0, matrix products: 39.7 us -> none  [the longest x3 19.4 us: per_device(): jnp.dot(tap_inputs[2], weights[2], preferred_element_type=jnp.float32)]
    ppermute x6 -> x0, starting transfers between devices: 15.7 us -> none  [shifted(): return lax.ppermute(array, axis, pairs)]
    convert_element_type x1 -> x0, other arithmetic: 5.32 us -> none  [per_device(): activated = jax.nn.gelu(stream.astype(jnp.float32) * pre_scale[layer_inde...]
    slice x4 -> x0, local copies, waits for them, and re-layouts: 4.2 us -> none  [the longest x2 3.28 us: neighbours(): to_prev = source[:dilation]]
  transfers between devices with their start and end apart: 9 -> 0, of which waited for: 7 -> 0; matrix products, arithmetic and copies ran while one was open for 6% -> 0% of each run, Pallas kernels for 0% -> 0%
where the time goes in v1:
time: 95.8 us; the launch traced here: 95.6 us
  Pallas kernels  93.5 us (98%)
  local copies, waits for them, and re-layouts  2.09 us (2%)
    pallas_call x1, Pallas kernels, per_device(): pl.pallas_call(functools.partial(kernel, n), out_shape=jax.ShapeDtypeStru...  93.5 us
    unnamed x1, local copies, waits for them, and re-layouts  2.09 us

profile of v1, /device:TPU:0, one launch (start us, length us, event | category | flops | bytes accessed | tf_op | source)
XLA Modules:
  0.0 95.6 jit_solution(1950148564802177288)
XLA Ops:
  0.0 93.5 %shard_map.55 = bf16[1024,384]{1,0:T(8,128)(2,1)} custom-call(bf16[1024,384]{1,0:T(8,128)(2,1)} %x_ref.1, f32[3,384]{1,0:T(4,128)} %scale_ref.1, f32[3,384]{1,0:T(4,128)} %shift_ref.1, bf16[3,3,1536,384]{3,2,1,0:T(8,128)(2,1)} %w_hbm.1, f32[3,384]{1,0:T(4,128)} %bias_ref.1), custom_call_target="tpu_custom_call" | custom-call | flops 10871635968 | bytes 10616832 | tf_op jit(solution)/shard_map/pallas_call | solution.py:238
  93.5 2.1 %copy.7 = bf16[1024,384]{1,0:T(8,128)(2,1)} copy(bf16[1024,384]{1,0:T(8,128)(2,1)} %shard_map.55) | data formatting | bytes 1572864

commit v2 on v1

--- a/solution.py
+++ b/solution.py
@@ -10,15 +10,19 @@
 LAYERS = 3
 SPACINGS = (64, 512, 4096)
 PIECES = 4
+FAR_ORDER = (2, 0, 3, 1)
+RAW = 3
 MESH = pl.DeviceIdType.MESH
 INV_SQRT2 = 0.7071067811865476
 
 
 def kernel(
     n, x_ref, scale_ref, shift_ref, w_hbm, bias_ref, out_ref,
-    full, w, acc, part, up_out, down_out, low_in, high_in,
+    full, w, acc, part, up_out, down_out, low_in, high_in, far,
     w_sem, core_send, core_recv, y_send, y_recv, fwd_send, fwd_recv,
     up_send, up_recv, down_send, down_recv,
+    raw_send, raw_recv, far_core_send, far_core_recv, far_y_send, far_y_recv,
+    far_fwd_send, far_fwd_recv,
 ):
     rows, width = x_ref.shape
     piece = rows // PIECES
@@ -27,10 +31,18 @@
     core = c + 1 - 2 * lax.rem(c, 2)
     across = lax.rem(c + 2, 4)
     hops = [max(1, d // rows) for d in SPACINGS]
-    rims = [min(d, rows) for d in SPACINGS]
+    rims = [d if d < rows else piece for d in SPACINGS]
     starts = [sum(rims[:l]) for l in range(LAYERS)]
     has_up = [s + h < n for h in hops]
     has_down = [s >= h for h in hops]
+
+    near = lax.div(c, 2)
+
+    def chip(index):
+        return pl.ds(pl.multiple_of(index * (2 * width), 2 * width), 2 * width)
+
+    def dot(a, b):
+        return jnp.dot(a, b, preferred_element_type=jnp.float32)
 
     def columns(index):
         return pl.ds(pl.multiple_of(index * width, width), width)
@@ -90,7 +102,57 @@
         y_copy(l, j).wait_recv()
         fwd_copy(l, j).start()
         core_copy(l, j).wait_recv()
-        fwd_copy(l, j).wait_recv()
+
+    last = LAYERS - 1
+    far_on = (has_down[last], has_up[last])
+
+    def raw_copy(side, p):
+        to = s + hops[last] if side == 0 else s - hops[last]
+        return pltpu.make_async_remote_copy(
+            block(last, FAR_ORDER[p], c), far.at[side, span(p), columns(c)],
+            raw_send.at[side, p], raw_recv.at[side, p],
+            device_id={"seq": to}, device_id_type=MESH)
+
+    def far_copy(side, p, owner, send_sem, recv_sem, to):
+        ref = far.at[side, span(p), columns(owner)]
+        return pltpu.make_async_remote_copy(
+            ref, ref, send_sem.at[side, p], recv_sem.at[side, p],
+            device_id={"ch": to}, device_id_type=MESH)
+
+    def far_core(side, p):
+        return far_copy(side, p, c, far_core_send, far_core_recv, core)
+
+    def far_y(side, p):
+        return far_copy(side, p, c, far_y_send, far_y_recv, across)
+
+    def far_fwd(side, p):
+        return far_copy(side, p, across, far_fwd_send, far_fwd_recv, core)
+
+    def send_raw(p):
+        for side, on in ((0, has_up[last]), (1, has_down[last])):
+            @pl.when(on)
+            def _():
+                raw_copy(side, p).start()
+
+    def relay(p):
+        for side in range(2):
+            @pl.when(far_on[side])
+            def _():
+                raw_copy(side, p).wait_recv()
+                far_y(side, p).start()
+                far_core(side, p).start()
+
+    def add_far(p):
+        for side in range(2):
+            @pl.when(far_on[side])
+            def _():
+                far_y(side, p).wait_recv()
+                far_fwd(side, p).start()
+                far_core(side, p).wait_recv()
+                at = span(FAR_ORDER[p])
+                acc[at, :] += dot(far[side, span(p), chip(near)], w[last, 2 * side, chip(near), :])
+                far_fwd(side, p).wait_recv()
+                acc[at, :] += dot(far[side, span(p), chip(1 - near)], w[last, 2 * side, chip(1 - near), :])
 
     def rim_rows(l, p):
         size = min(piece, rims[l])
@@ -132,21 +194,30 @@
             down_copy(l, p).wait_recv()
             acc[at, :] += high_in[rim_rows(l, p), :].astype(jnp.float32)
 
-    def product(l, j, k):
-        return jnp.dot(full[l, span(j), :], w[l, k], preferred_element_type=jnp.float32)
+    def product(l, j, k, index):
+        return dot(full[l, span(j), chip(index)], w[l, k, chip(index), :])
 
     def step(l, j):
         arrive(l, j)
         d = SPACINGS[l]
         if d >= rows:
-            send_up(l, j, lambda: product(l, j, 0))
-            send_down(l, j, lambda: product(l, j, 2))
-            acc[span(j), :] += product(l, j, 1)
+            acc[span(j), :] += product(l, j, 1, near)
+            fwd_copy(l, j).wait_recv()
+            if FAR_ORDER.index(j) >= RAW:
+                send_up(l, 0, lambda: product(l, j, 0, near) + product(l, j, 0, 1 - near))
+                send_down(l, 0, lambda: product(l, j, 2, near) + product(l, j, 2, 1 - near))
+            acc[span(j), :] += product(l, j, 1, 1 - near)
             return
 
         @pl.loop(0, 3)
         def _(k):
-            part[k] = product(l, j, k)
+            part[k] = product(l, j, k, near)
+
+        fwd_copy(l, j).wait_recv()
+
+        @pl.loop(0, 3)
+        def _(k):
+            part[k] += product(l, j, k, 1 - near)
 
         first = j * piece
         inside = max(0, min(piece, rows - d - first))
@@ -162,20 +233,24 @@
             acc[pl.ds(first + outside - d, piece - outside), :] += part[2, outside:piece]
 
     def finish(l, j):
-        d = SPACINGS[l]
         first = j * piece
         size = min(piece, rims[l])
+        if l == last:
+            if FAR_ORDER.index(j) >= RAW:
+                take_low(l, 0, span(j))
+                take_high(l, 0, span(j))
+            out_ref[span(j), :] = acc[span(j), :].astype(jnp.bfloat16)
+            return
         if first < rims[l]:
             take_low(l, first // size, pl.ds(first, size))
         if first + piece > rows - rims[l]:
             at = max(first, rows - rims[l])
             take_high(l, (at - (rows - rims[l])) // size, pl.ds(at, size))
         value = acc[span(j), :].astype(jnp.bfloat16)
-        if l == LAYERS - 1:
-            out_ref[span(j), :] = value
-        else:
-            activate(l + 1, j, value.astype(jnp.float32))
-            send(l + 1, j)
+        activate(l + 1, j, value.astype(jnp.float32))
+        if l + 1 == last and FAR_ORDER.index(j) < RAW:
+            send_raw(FAR_ORDER.index(j))
+        send(l + 1, j)
 
     activate(0, 3, x_ref[span(3), :].astype(jnp.float32))
     met = 2
@@ -208,11 +283,32 @@
     finish(1, 1)
 
     w_copies[2].wait()
-    for j in (2, 0, 3, 1):
-        step(2, j)
-    for j in (2, 0, 3, 1):
-        finish(2, j)
-
+    step(2, 2)
+    relay(0)
+    step(2, 0)
+    step(2, 3)
+    relay(1)
+    step(2, 1)
+    add_far(0)
+    finish(2, 2)
+    relay(2)
+    add_far(1)
+    finish(2, 0)
+    add_far(2)
+    finish(2, 3)
+    finish(2, 1)
+
+    for p in range(RAW):
+        for side, on in ((0, has_up[last]), (1, has_down[last])):
+            @pl.when(on)
+            def _():
+                raw_copy(side, p).wait_send()
+
+            @pl.when(far_on[side])
+            def _():
+                far_y(side, p).wait_send()
+                far_core(side, p).wait_send()
+                far_fwd(side, p).wait_send()
     for l in range(LAYERS):
         for j in range(PIECES):
             y_copy(l, j).wait_send()
@@ -231,7 +327,7 @@
 def per_device(n, bins_in, pre_scale, pre_shift, conv_weight, conv_bias):
     rows, width = bins_in.shape
     depth = conv_weight.shape[2]
-    rim_total = sum(min(d, rows) for d in SPACINGS)
+    rim_total = sum(d if d < rows else rows // PIECES for d in SPACINGS)
     vmem = pl.BlockSpec(memory_space=pltpu.VMEM)
     pair = pltpu.SemaphoreType.DMA((LAYERS, PIECES))
     rim = pltpu.VMEM((rim_total, width), jnp.bfloat16)
@@ -246,8 +342,9 @@
             pltpu.VMEM((rows, width), jnp.float32),
             pltpu.VMEM((3, rows // PIECES, width), jnp.float32),
             rim, rim, rim, rim,
+            pltpu.VMEM((2, RAW * rows // PIECES, depth), jnp.bfloat16),
             pltpu.SemaphoreType.DMA((LAYERS,)),
-        ] + [pair] * 10,
+        ] + [pair] * 10 + [pltpu.SemaphoreType.DMA((2, RAW))] * 8,
         compiler_params=pltpu.CompilerParams(
             collective_id=0, has_side_effects=True, vmem_limit_bytes=56 * 1024 * 1024
         ),

time: 95.8 us -> 96 us (level)
  the two profiles are of different devices: /device:TPU:0 before, /device:TPU:17 now
where the time goes in v2:
time: 96 us; the launch traced here: 95.8 us
  Pallas kernels  93.7 us (98%)
  local copies, waits for them, and re-layouts  2.09 us (2%)
    pallas_call x1, Pallas kernels, per_device(): pl.pallas_call(functools.partial(kernel, n), out_shape=jax.ShapeDtypeStru...  93.7 us
    unnamed x1, local copies, waits for them, and re-layouts  2.09 us

profile of v2, /device:TPU:17, one launch (start us, length us, event | category | flops | bytes accessed | tf_op | source)
XLA Modules:
  0.0 95.8 jit_solution(11401568562666392621)
XLA Ops:
  0.0 93.7 %shard_map.55 = bf16[1024,384]{1,0:T(8,128)(2,1)} custom-call(bf16[1024,384]{1,0:T(8,128)(2,1)} %x_ref.1, f32[3,384]{1,0:T(4,128)} %scale_ref.1, f32[3,384]{1,0:T(4,128)} %shift_ref.1, bf16[3,3,1536,384]{3,2,1,0:T(8,128)(2,1)} %w_hbm.1, f32[3,384]{1,0:T(4,128)} %bias_ref.1), custom_call_target="tpu_custom_call" | custom-call | flops 10871635968 | bytes 10616832 | tf_op jit(solution)/shard_map/pallas_call | solution.py:334
  93.7 2.1 %copy.7 = bf16[1024,384]{1,0:T(8,128)(2,1)} copy(bf16[1024,384]{1,0:T(8,128)(2,1)} %shard_map.55) | data formatting | bytes 1572864

commit v3 on v2

--- a/solution.py
+++ b/solution.py
@@ -11,7 +11,7 @@
 SPACINGS = (64, 512, 4096)
 PIECES = 4
 FAR_ORDER = (2, 0, 3, 1)
-RAW = 3
+RAW = 2
 MESH = pl.DeviceIdType.MESH
 INV_SQRT2 = 0.7071067811865476
 
@@ -31,15 +31,10 @@
     core = c + 1 - 2 * lax.rem(c, 2)
     across = lax.rem(c + 2, 4)
     hops = [max(1, d // rows) for d in SPACINGS]
-    rims = [d if d < rows else piece for d in SPACINGS]
+    rims = [d if d < rows else (PIECES - RAW) * piece for d in SPACINGS]
     starts = [sum(rims[:l]) for l in range(LAYERS)]
     has_up = [s + h < n for h in hops]
     has_down = [s >= h for h in hops]
-
-    near = lax.div(c, 2)
-
-    def chip(index):
-        return pl.ds(pl.multiple_of(index * (2 * width), 2 * width), 2 * width)
 
     def dot(a, b):
         return jnp.dot(a, b, preferred_element_type=jnp.float32)
@@ -102,6 +97,7 @@
         y_copy(l, j).wait_recv()
         fwd_copy(l, j).start()
         core_copy(l, j).wait_recv()
+        fwd_copy(l, j).wait_recv()
 
     last = LAYERS - 1
     far_on = (has_down[last], has_up[last])
@@ -149,10 +145,8 @@
                 far_y(side, p).wait_recv()
                 far_fwd(side, p).start()
                 far_core(side, p).wait_recv()
-                at = span(FAR_ORDER[p])
-                acc[at, :] += dot(far[side, span(p), chip(near)], w[last, 2 * side, chip(near), :])
                 far_fwd(side, p).wait_recv()
-                acc[at, :] += dot(far[side, span(p), chip(1 - near)], w[last, 2 * side, chip(1 - near), :])
+                acc[span(FAR_ORDER[p]), :] += dot(far[side, span(p), :], w[last, 2 * side])
 
     def rim_rows(l, p):
         size = min(piece, rims[l])
@@ -194,30 +188,23 @@
             down_copy(l, p).wait_recv()
             acc[at, :] += high_in[rim_rows(l, p), :].astype(jnp.float32)
 
-    def product(l, j, k, index):
-        return dot(full[l, span(j), chip(index)], w[l, k, chip(index), :])
+    def product(l, j, k):
+        return dot(full[l, span(j), :], w[l, k])
 
     def step(l, j):
         arrive(l, j)
         d = SPACINGS[l]
         if d >= rows:
-            acc[span(j), :] += product(l, j, 1, near)
-            fwd_copy(l, j).wait_recv()
-            if FAR_ORDER.index(j) >= RAW:
-                send_up(l, 0, lambda: product(l, j, 0, near) + product(l, j, 0, 1 - near))
-                send_down(l, 0, lambda: product(l, j, 2, near) + product(l, j, 2, 1 - near))
-            acc[span(j), :] += product(l, j, 1, 1 - near)
+            p = FAR_ORDER.index(j) - RAW
+            if p >= 0:
+                send_up(l, p, lambda: product(l, j, 0))
+                send_down(l, p, lambda: product(l, j, 2))
+            acc[span(j), :] += product(l, j, 1)
             return
 
         @pl.loop(0, 3)
         def _(k):
-            part[k] = product(l, j, k, near)
-
-        fwd_copy(l, j).wait_recv()
-
-        @pl.loop(0, 3)
-        def _(k):
-            part[k] += product(l, j, k, 1 - near)
+            part[k] = product(l, j, k)
 
         first = j * piece
         inside = max(0, min(piece, rows - d - first))
@@ -236,9 +223,10 @@
         first = j * piece
         size = min(piece, rims[l])
         if l == last:
-            if FAR_ORDER.index(j) >= RAW:
-                take_low(l, 0, span(j))
-                take_high(l, 0, span(j))
+            p = FAR_ORDER.index(j) - RAW
+            if p >= 0:
+                take_low(l, p, span(j))
+                take_high(l, p, span(j))
             out_ref[span(j), :] = acc[span(j), :].astype(jnp.bfloat16)
             return
         if first < rims[l]:
@@ -284,17 +272,15 @@
 
     w_copies[2].wait()
     step(2, 2)
-    relay(0)
     step(2, 0)
     step(2, 3)
+    relay(0)
+    step(2, 1)
     relay(1)
-    step(2, 1)
     add_far(0)
     finish(2, 2)
-    relay(2)
     add_far(1)
     finish(2, 0)
-    add_far(2)
     finish(2, 3)
     finish(2, 1)
 
@@ -327,7 +313,7 @@
 def per_device(n, bins_in, pre_scale, pre_shift, conv_weight, conv_bias):
     rows, width = bins_in.shape
     depth = conv_weight.shape[2]
-    rim_total = sum(d if d < rows else rows // PIECES for d in SPACINGS)
+    rim_total = sum(d if d < rows else (PIECES - RAW) * rows // PIECES for d in SPACINGS)
     vmem = pl.BlockSpec(memory_space=pltpu.VMEM)
     pair = pltpu.SemaphoreType.DMA((LAYERS, PIECES))
     rim = pltpu.VMEM((rim_total, width), jnp.bfloat16)

time: 96 us -> 94.5 us (0.984)
  the two profiles are of different devices: /device:TPU:17 before, /device:TPU:0 now
where the time goes in v3:
time: 94.5 us; the launch traced here: 94 us
  Pallas kernels  91.9 us (97%)
  local copies, waits for them, and re-layouts  2.09 us (2%)
    pallas_call x1, Pallas kernels, per_device(): pl.pallas_call(functools.partial(kernel, n), out_shape=jax.ShapeDtypeStru...  91.9 us
    unnamed x1, local copies, waits for them, and re-layouts  2.09 us

profile of v3, /device:TPU:0, one launch (start us, length us, event | category | flops | bytes accessed | tf_op | source)
XLA Modules:
  0.0 94.0 jit_solution(7651642052807026147)
XLA Ops:
  0.0 91.9 %shard_map.55 = bf16[1024,384]{1,0:T(8,128)(2,1)} custom-call(bf16[1024,384]{1,0:T(8,128)(2,1)} %x_ref.1, f32[3,384]{1,0:T(4,128)} %scale_ref.1, f32[3,384]{1,0:T(4,128)} %shift_ref.1, bf16[3,3,1536,384]{3,2,1,0:T(8,128)(2,1)} %w_hbm.1, f32[3,384]{1,0:T(4,128)} %bias_ref.1), custom_call_target="tpu_custom_call" | custom-call | flops 10871635968 | bytes 10616832 | tf_op jit(solution)/shard_map/pallas_call | solution.py:320
  91.9 2.1 %copy.7 = bf16[1024,384]{1,0:T(8,128)(2,1)} copy(bf16[1024,384]{1,0:T(8,128)(2,1)} %shard_map.55) | data formatting | bytes 1572864
